TPU v7x, 256 devices: a whole 4x4x8 slice. The times are simulated.
256 devices in a mesh: img: 16 (over x, y_lo, core), patch: 16 (over z, y_hi).
Axes of the slice: x: 4, y: 4 (y_hi: 2, y_lo: 2; y = y_hi * 2 + y_lo), z: 8, core: 2. Of those that a mesh axis runs over, the one named last changes fastest.
Arguments:
- img_q: bfloat16 [16, 2048, 1536], P('img', 'patch')
- fresh_kv: bfloat16 [16, 2048, 3072], P('img', 'patch'), may hold values from -6 to 6
- stale_kv: bfloat16 [16, 2048, 3072], P('img', 'patch')
- text_states: bfloat16 [16, 512, 4096], P('img', 'patch'), may hold values from -6 to 6
- ctx_weight: bfloat16 [4096, 3072], P('img', 'patch'), may hold values from -0.09375 to 0.09375
- kv_weight: bfloat16 [3072, 3072], P('img', 'patch'), may hold values from -0.109375 to 0.109375
- modulation: float32 [16, 2, 3072], P('img', None, 'patch'), may hold values from -3 to 3
- lengths: int32 [16], P('img'), may hold values from 1 to 512, as said below
Outputs:
- attended: bfloat16 [16, 2048, 1536], P('img', 'patch')
Inputs may be any that keep to these rules, and one draw needn't show every extreme that they name: `lengths`: every length is at least 1 and some image's prompt has 512 live tokens.
All inputs are finite; a program needn't handle non-finite values.
Results may differ from a plain program's by a relative error of at most 0.012.
Values may be sent and summed in bfloat16 or wider, within the bound.
A program may use at most 128 MiB of HBM per device.

v0:
```python
import math

import jax
import jax.numpy as jnp
from jax import lax
from jax.sharding import PartitionSpec as P

D = 3072
HEAD = 128


def split_heads(kv_rows, head_count):
    count_rows = kv_rows.shape[0]
    hd_width = head_count * HEAD
    key_heads = kv_rows[:, :hd_width].reshape(count_rows, head_count, HEAD)
    value_heads = kv_rows[:, hd_width:].reshape(count_rows, head_count, HEAD)
    return (key_heads, value_heads)


def per_device(img_q, fresh_kv, stale_kv, text_states, ctx_weight, kv_weight, modulation, lengths):
    row_count = img_q.shape[1]
    hd_width = img_q.shape[2]
    head_count = hd_width // HEAD
    scaling = 1.0 / math.sqrt(HEAD)
    prompt = lax.all_gather(text_states, "patch", axis=1, tiled=True)[0]
    ctx_full, kv_full = (
        lax.all_gather(ctx_weight, "img", axis=0, tiled=True),
        lax.all_gather(kv_weight, "img", axis=0, tiled=True),
    )
    context = jnp.dot(prompt, ctx_full, preferred_element_type=jnp.float32)
    feature_sum, squares = lax.psum((jnp.sum(context, -1), jnp.sum(context * context, -1)), "patch")
    average = feature_sum[:, None] / D
    variance = squares[:, None] / D - average * average
    modul = modulation[0]
    normed = (
        (context - average) * lax.rsqrt(variance + 1e-06) * (1.0 + modul[0]) + modul[1]
    ).astype(jnp.bfloat16)
    contract = (((1,), (1,)), ((), ()))
    partial_kv = lax.dot_general(normed, kv_full, contract, preferred_element_type=jnp.float32)
    text_kv = lax.psum(partial_kv.astype(jnp.bfloat16), "patch")
    queries = img_q[0].reshape(row_count, head_count, HEAD)
    first_kv = jnp.concatenate([text_kv, fresh_kv[0]], 0)
    key_heads, value_heads = split_heads(first_kv, head_count)
    text_count = text_kv.shape[0]
    usable = jnp.concatenate(
        [jnp.arange(text_count, dtype=jnp.int32) < lengths[0], jnp.ones((row_count,), jnp.bool_)]
    )
    scores = (
        jnp.einsum("rhd,nhd->rhn", queries, key_heads, preferred_element_type=jnp.float32) * scaling
    )
    scores = jnp.where(usable[None, None, :], scores, -jnp.inf)
    highest = jnp.max(scores, -1)
    weights = jnp.exp(scores - highest[..., None])
    denom = jnp.sum(weights, -1)
    summed = jnp.einsum(
        "rhn,nhd->rhd",
        weights.astype(jnp.bfloat16),
        value_heads,
        preferred_element_type=jnp.float32,
    )
    own_start = lax.axis_index("patch") * row_count
    old_sum = summed
    key_block = lax.all_gather(stale_kv, "patch", axis=1, tiled=True)[0]
    block_keys, block_values = split_heads(key_block, head_count)
    block_scores = (
        jnp.einsum("rhd,nhd->rhn", queries, block_keys, preferred_element_type=jnp.float32)
        * scaling
    )
    position = jnp.arange(key_block.shape[0], dtype=jnp.int32)
    outside = (position < own_start) | (position >= own_start + row_count)
    block_scores = jnp.where(outside[None, None, :], block_scores, -jnp.inf)
    new_max = jnp.maximum(highest, jnp.max(block_scores, -1))
    rescale = jnp.exp(highest - new_max)
    block_weights = jnp.exp(block_scores - new_max[..., None])
    new_denom = denom * rescale + jnp.sum(block_weights, -1)
    added = jnp.einsum(
        "rhn,nhd->rhd",
        block_weights.astype(jnp.bfloat16),
        block_values,
        preferred_element_type=jnp.float32,
    )
    summed = old_sum * rescale[..., None] + added
    attended = (summed / new_denom[..., None]).reshape(row_count, hd_width).astype(jnp.bfloat16)
    return attended[None]


def solution(mesh):
    in_specs = (
        P("img", "patch", None),
        P("img", "patch", None),
        P("img", "patch", None),
        P("img", "patch", None),
        P("img", "patch"),
        P("img", "patch"),
        P("img", None, "patch"),
        P("img"),
    )
    out_specs = P("img", "patch", None)
    return jax.shard_map(
        per_device, mesh=mesh, in_specs=in_specs, out_specs=out_specs, check_vma=False
    )
```

profile of v0, /device:TPU:2, one launch (start us, length us, event | category | flops | bytes accessed | tf_op | source)
XLA Modules:
  0.0 601.3 jit_solution(17004250352739703591)
XLA Ops:
  6.5 0.0 all-gather.7.cloned.1.call-start
  6.5 0.7 all-gather.7.cloned.1.call-update
  7.3 0.0 all-gather.5.cloned.1.call-start
  7.3 0.7 all-gather.5.cloned.1.call-update
  8.0 0.0 all-gather.9.cloned.1.call-start
  8.1 0.7 all-gather.9.cloned.1.call-update
  8.7 0.0 all-reduce.4.cloned.1.call-start
  8.8 0.8 slice_add_fusion
  9.5 40.4 %all-gather.7.cloned.1.call-done = bf16[4096,192]{0,1:T(8,128)(2,1)} async-done(((bf16[256,192]{0,1:T(8,128)(2,1)}), bf16[4096,192]{0,1:T(8,128)(2,1)}) %all-gather.7.cloned.1.call-update) | async-done | bytes 1572880 | tf_op jit(solution)/shard_map/all_gather | solution.py:27
  50.0 102.9 %all-gather.5.cloned.1.call-done = bf16[1,512,4096]{2,1,0:T(8,128)(2,1)} async-done(((bf16[1,32,4096]{2,1,0:T(8,128)(2,1)}), bf16[1,512,4096]{2,1,0:T(8,128)(2,1)}) %all-gather.5.cloned.1.call-update) | async-done | bytes 4194320 | tf_op jit(solution)/shard_map/all_gather | solution.py:25
  152.9 4.2 fusion.48
  157.1 38.6 %all-reduce.1 = (f32[512]{0:T(512)S(1)}, f32[512]{0:T(512)S(1)}) all-reduce(f32[512]{0:T(512)S(1)} %get-tuple-element.6, f32[512]{0:T(512)S(1)} %get-tuple-element.5), channel_id=1, replica_groups=mesh['img'=16,'patch'=16] {'patch'}, use_global_device_ids=true, to_apply=%region_3.0 | all-reduce | flops 1024 | bytes 8192 | tf_op jit(solution)/shard_map/psum | solution.py:31
  195.7 0.0 all-gather.9.cloned.1.call-done
  195.7 0.0 copy-start.3
  195.8 4.3 convolution_convert_fusion
  200.1 0.0 copy-start.5
  200.1 0.0 copy-start.4
  200.1 0.0 all-reduce.4.cloned.1.call-update
  200.1 0.0 all-gather.11.cloned.1.call-start
  200.1 0.0 copy-done.3
  200.1 1.2 copy.23
  201.4 0.0 all-gather.11.cloned.1.call-update
  201.4 0.0 copy-done.5
  201.4 0.2 copy.19
  202.3 174.6 %all-reduce.4.cloned.1.call-done = bf16[512,3072]{1,0:T(8,128)(2,1)} async-done(((bf16[512,3072]{1,0:T(8,128)(2,1)}), bf16[512,3072]{1,0:T(8,128)(2,1)}) %all-reduce.4.cloned.1.call-update) | async-done | bytes 3145744 | tf_op jit(solution)/shard_map/psum | solution.py:40
  376.9 0.0 copy-done.4
  376.9 5.7 fusion.16
  382.6 2.8 copy.18
  385.4 4.0 copy.17
  389.4 1.1 bitcast_reduce_fusion.1
  390.5 0.0 copy-start
  390.5 1.9 copy-done
  392.4 0.9 fusion.12
  393.3 176.1 %all-gather.11.cloned.1.call-done = bf16[1,2048,3072]{1,2,0:T(8,128)(2,1)} async-done(((bf16[1,128,3072]{1,2,0:T(8,128)(2,1)}), bf16[1,2048,3072]{1,2,0:T(8,128)(2,1)}) %all-gather.11.cloned.1.call-update) | async-done | bytes 12582928 | tf_op jit(solution)/shard_map/all_gather | solution.py:63
  569.4 8.5 %fusion.49 = (bf16[2048,1536]{0,1:T(8,128)(2,1)S(1)}, bf16[2048,1536]{0,1:T(8,128)(2,1)}) fusion(bf16[2048,3072]{0,1:T(8,128)(2,1)} %bitcast.70), kind=kLoop, calls=%fused_computation.55 | loop fusion | bytes 25165824 | tf_op jit(solution)/shard_map/slice | solution.py:15
  577.9 3.6 bitcast_reduce_fusion
  581.6 3.5 fusion.1
  585.1 0.0 copy-start.1
  585.1 0.0 copy-start.2
  585.1 7.3 %fusion.24 = f32[128,12,128]{0,2,1:T(8,128)S(1)} fusion(bf16[2048,12,128]{0,2,1:T(8,128)(2,1)} %bitcast.72, f32[12,2048,128]{2,1,0:T(8,128)S(1)} %get-tuple-element.23, f32[128,12]{0,1:T(8,128)S(1)} %max.13, pred[2048]{0:T(1024)(128)(4,1)S(1)} %fusion.43), kind=kOutput, calls=%fused_computation.30 | convolution fusion | flops 817889280 | bytes 19668992 | tf_op jit(solution)/shard_map/rhn,nhd->rhd/dot_general | solution.py:76
  592.5 0.0 copy-done.1
  592.5 0.0 copy-done.2
  592.5 1.4 fusion.36
  593.9 0.9 copy.27
  (6 shorter events, 0.0 us)
Async XLA Ops:
  6.5 43.4 %all-gather.7.cloned.1.call-start = ((), (), s32[]{:S(2)}) async-start(), calls=%async_computation.1 | async-start | bytes 1671168 | tf_op jit(solution)/shard_map/all_gather | solution.py:27
  7.3 145.6 %all-gather.5.cloned.1.call-start = ((), (), s32[]{:S(2)}) async-start(), calls=%async_computation | async-start | bytes 4456448 | tf_op jit(solution)/shard_map/all_gather | solution.py:25
  8.0 187.7 %all-gather.9.cloned.1.call-start = ((), (), s32[]{:S(2)}) async-start(), calls=%async_computation.2 | async-start | bytes 1671168 | tf_op jit(solution)/shard_map/all_gather | solution.py:28
  8.7 368.2 %all-reduce.4.cloned.1.call-start = ((), (), s32[]{:S(2)}) async-start(), calls=%async_computation.3 | async-start | bytes 6291456 | tf_op jit(solution)/shard_map/psum | solution.py:40
  195.7 4.4 copy-start.3
  200.1 1.4 copy-start.5
  200.1 176.9 %copy-start.4 = (bf16[1,128,3072]{2,1,0:T(8,128)(2,1)S(1)}, bf16[1,128,3072]{2,1,0:T(8,128)(2,1)}, u32[]{:S(2)}) copy-start(bf16[1,128,3072]{2,1,0:T(8,128)(2,1)} %param.9) | copy-start | bytes 2359300
  200.1 369.3 %all-gather.11.cloned.1.call-start = ((), (), s32[]{:S(2)}) async-start(), calls=%async_computation.4 | async-start | bytes 13369344 | tf_op jit(solution)/shard_map/all_gather | solution.py:63
  390.5 1.9 copy-start
  585.1 7.4 %copy-start.1 = (f32[12,640,128]{2,1,0:T(8,128)S(1)}, f32[12,640,128]{2,1,0:T(8,128)}, u32[]{:S(2)}) copy-start(f32[12,640,128]{2,1,0:T(8,128)} %copy-done) | copy-start | bytes 11796484
  585.1 7.4 %copy-start.2 = (bf16[640,1536]{0,1:T(8,128)(2,1)S(1)}, bf16[640,1536]{0,1:T(8,128)(2,1)}, u32[]{:S(2)}) copy-start(bf16[640,1536]{0,1:T(8,128)(2,1)} %copy.17) | copy-start | bytes 5898244
Sparse Core Ops, SparseCore 0:
  9.1 40.7 all-gather.6
  52.5 100.2 all-gather.4
  154.7 31.8 all-gather.8
  200.2 176.6 all-reduce.3
  379.2 190.1 all-gather.10
where the time goes:
time: 602 us; the launch traced here: 601 us
  waiting for transfers between devices  496 us (82%)
  blocking collectives  38.6 us (6%)
  matrix products  21.9 us (4%)
  local copies, waits for them, and re-layouts  19.7 us (3%)
  between operations  14 us (2%)
  other arithmetic  10.9 us (2%)
    all_gather x1, waiting for transfers between devices, per_device(): key_block = lax.all_gather(stale_kv, 'patch', axis=1, tiled=True)[0]  176 us
    psum x1, waiting for transfers between devices, per_device(): text_kv = lax.psum(partial_kv.astype(jnp.bfloat16), 'patch')  175 us
    all_gather x1, waiting for transfers between devices, per_device(): prompt = lax.all_gather(text_states, 'patch', axis=1, tiled=True)[0]  103 us
    all_gather x1, waiting for transfers between devices, per_device(): lax.all_gather(ctx_weight, 'img', axis=0, tiled=True)  40.4 us
    psum x1, blocking collectives, per_device(): lax.psum((jnp.sum(context, -1), jnp.sum(context * context, -1)), 'patch')  38.6 us
  transfers between devices with their start and end apart: 5, of which 4 were waited for; matrix products, arithmetic and copies ran while one was open for 3% of the time, Pallas kernels for 0%

commit v1 on v0

v1 whole, which is shorter than its diff:
```python
import functools
import math

import jax
import jax.numpy as jnp
from jax import lax
from jax.experimental import pallas as pl
from jax.experimental.pallas import tpu as pltpu
from jax.sharding import PartitionSpec as P

D = 3072
HEAD = 128
NX, NY, NZ = 4, 4, 8
HALF = 768
NH = 6
MESH = pl.DeviceIdType.MESH
BF = jnp.bfloat16
F32 = jnp.float32


def device(x, y, z, core):
    return ((x * 2 + y % 2) * 2 + core, z * 2 + y // 2)


class Net:
    def __init__(self, send, recv):
        self.send, self.recv, self.used, self.copies = send, recv, 0, []

    def copy(self, src, dst, to):
        n = self.used
        self.used += 1
        c = pltpu.make_async_remote_copy(
            src_ref=src,
            dst_ref=dst,
            send_sem=self.send.at[n],
            recv_sem=self.recv.at[n],
            device_id=to,
            device_id_type=MESH,
        )
        self.copies.append(c)
        return c

    def drain(self):
        for c in self.copies:
            c.wait_send()


class Ring:
    def __init__(self, net, slot, rows, left, right, first=None, by_origin=False):
        h = rows // 2
        self.step = {}
        for s in range(4):
            for way in (0, 1):
                if way == 0:
                    a, b, to, part = s, s + 1, right, pl.ds(0, h)
                else:
                    a, b, to, part = (8 - s) % 8, 7 - s, left, pl.ds(h, h)
                src, dst = slot(a), slot(a if by_origin else b)
                if s == 0 and first is not None:
                    src = first
                if s == 3:
                    src, dst = src.at[part], dst.at[part]
                self.step[way, s] = net.copy(src, dst, to)

    def start(self):
        self.step[0, 0].start()
        self.step[1, 0].start()

    def forward(self, s):
        for way in (0, 1):
            self.step[way, s - 1].wait_recv()
            self.step[way, s].start()

    def finish(self):
        for way in (0, 1):
            self.step[way, 3].wait_recv()


def kernel(
    q_hbm, fresh_hbm, stale_hbm, text_hbm, cw_ref, kw_ref, mod_ref, len_ref, out_ref,
    tx, wy, ky, wx, kx, mb, st, pt, rs_out, rs_in, tkv, tk, tv, sk, sv, qb, fk, fv,
    acc, mx, dn, ob, ob_in, send_sem, recv_sem, loc_sem,
):
    img, patch = lax.axis_index("img"), lax.axis_index("patch")
    x, core = img // 4, img % 2
    z, h = patch // 2, patch % 2
    y = h * 2 + (img // 2) % 2
    right, left = device(x, y, (z + 1) % NZ, core), device(x, y, (z + 7) % NZ, core)
    zs = {k: device(x, y, (z + k) % NZ, core) for k in range(1, NZ)}
    xs = {k: device((x + k) % NX, y, z, core) for k in range(1, NX)}
    ys = {k: device(x, (y + k) % NY, z, core) for k in range(1, NY)}
    other = device(x, y, z, 1 - core)
    opposite = ys[2]
    mine, theirs = h * HALF, (1 - h) * HALF
    net = Net(send_sem, recv_sem)

    def at_z(k):
        return (z + NZ - k) % NZ

    def cols(ref, at):
        return ref.at[0, :, pl.ds(pl.multiple_of(at, 128), HALF)]

    locals_ = []

    def local(src, dst):
        c = pltpu.make_async_copy(src, dst, loc_sem.at[len(locals_)])
        locals_.append(c)
        c.start()
        return c

    c_text = local(text_hbm.at[0], tx.at[z])
    c_q = local(cols(q_hbm, mine), qb.at[0])
    c_fk = local(cols(fresh_hbm, mine), fk.at[0])
    c_fv = local(cols(fresh_hbm, D // 2 + mine), fv.at[0])
    c_sk = local(cols(stale_hbm, mine), sk.at[0, 0])
    c_sv = local(cols(stale_hbm, D // 2 + mine), sv.at[0, 0])

    w = cw_ref[...]
    wy[y, 0:256] = w[:, 0:128]
    wy[y, 256:384] = jnp.concatenate([w[0:128, 128:192], w[128:256, 128:192]], axis=1)
    w = kw_ref[...]
    ky[y, 0:192] = w[:, 0:128]
    ky[y, 192:288] = jnp.concatenate([w[0:96, 128:192], w[96:192, 128:192]], axis=1)
    mb[h, 0:2, 0:192] = mod_ref[0]

    barrier = pltpu.get_barrier_semaphore()
    peers = [*zs.values(), *xs.values(), *ys.values(), other]
    for d in peers:
        pl.semaphore_signal(barrier, inc=1, device_id=d, device_id_type=MESH)
    pl.semaphore_wait(barrier, len(peers))

    text = Ring(net, lambda k: tx.at[at_z(k)], 32, left, right, text_hbm.at[0], True)
    text.start()
    wy_c = {k: net.copy(wy.at[y], wy.at[y], ys[k]) for k in ys}
    ky_c = {k: net.copy(ky.at[y], ky.at[y], ys[k]) for k in ys}
    for c in wy_c.values():
        c.start()
    m_c = net.copy(mb.at[h], mb.at[h], opposite)
    m_c.start()
    for c in ky_c.values():
        c.start()

    s_opp = [
        net.copy(cols(stale_hbm, theirs), sk.at[0, 1], opposite),
        net.copy(cols(stale_hbm, D // 2 + theirs), sv.at[0, 1], opposite),
    ]
    qf_opp = [
        net.copy(cols(q_hbm, theirs), qb.at[1], opposite),
        net.copy(cols(fresh_hbm, theirs), fk.at[1], opposite),
        net.copy(cols(fresh_hbm, D // 2 + theirs), fv.at[1], opposite),
    ]
    stale = [
        Ring(net, lambda k, b=b, r=r: b.at[k, r], 128, left, right, first=f)
        for r in (0, 1)
        for b, f in (
            (sk, cols(stale_hbm, mine) if r == 0 else None),
            (sv, cols(stale_hbm, D // 2 + mine) if r == 0 else None),
        )
    ]

    def pair(tiles, rows, out):
        for lo in (0, 1):
            a, b = tiles[lo], tiles[2 + lo]
            out[x, core, lo, 0] = a[0:rows]
            out[x, core, lo, 1] = b[0:rows]
            a, b = a[rows:], b[rows:]
            out[x, core, lo, 2, 0 : rows // 2] = jnp.concatenate([a[:, 0:64], b[:, 0:64]], axis=1)
            out[x, core, lo, 2, rows // 2 :] = jnp.concatenate([a[:, 64:], b[:, 64:]], axis=1)

    def spread(got, tiles, rows, out):
        for c in got.values():
            c.wait_recv()
        pair(tiles, rows, out)
        to_x = {k: net.copy(out.at[x, core], out.at[x, core], xs[k]) for k in xs}
        for c in to_x.values():
            c.start()
        to_core = [net.copy(out.at[x, core], out.at[x, core], other)]
        to_core[0].start()
        for k in xs:
            at = (x + NX - k) % NX
            to_core.append(net.copy(out.at[at, core], out.at[at, core], other))
        return to_x, to_core

    def pass_on(to_x, to_core, k):
        to_x[k].wait_recv()
        to_core[k].start()

    wx_x, wx_core = spread(wy_c, wy, 256, wx)
    for c in s_opp:
        c.start()
    text.forward(1)
    stale[0].start()
    stale[1].start()
    for c in qf_opp:
        c.start()
    kx_x, kx_core = spread(ky_c, ky, 192, kx)
    text.forward(2)
    pass_on(wx_x, wx_core, 1)
    pass_on(wx_x, wx_core, 3)
    text.forward(3)
    pass_on(wx_x, wx_core, 2)
    stale[0].forward(1)
    stale[1].forward(1)
    for c in s_opp:
        c.wait_recv()
    stale[2].start()
    stale[3].start()
    text.finish()
    c_text.wait()
    for c in wx_core:
        c.wait_recv()

    ctx = jnp.zeros((256, 384), F32)
    for i in range(NX):
        rhs = jnp.concatenate(
            [
                jnp.concatenate([wx[i, c, lo, b] for b in range(3)], axis=1)
                for lo in (0, 1)
                for c in (0, 1)
            ],
            axis=0,
        )
        lhs = tx[:, :, i * 1024 : (i + 1) * 1024].reshape(256, 1024)
        ctx = ctx + jnp.dot(lhs, rhs, preferred_element_type=F32)
    lane = lax.broadcasted_iota(jnp.int32, (256, 128), 1)
    s1 = jnp.sum(ctx, -1, keepdims=True)
    s2 = jnp.sum(ctx * ctx, -1, keepdims=True)
    both = jnp.where(lane == 0, s1, jnp.where(lane == 1, s2, 0.0))
    st[0] = jnp.transpose(both)[0:8]
    st_c = [net.copy(st.at[0], st.at[k], zs[k]) for k in zs]
    for c in st_c:
        c.start()
    pass_on(kx_x, kx_core, 1)
    pass_on(kx_x, kx_core, 3)
    pass_on(kx_x, kx_core, 2)
    m_c.wait_recv()
    low = lax.broadcasted_iota(jnp.int32, (8, 128), 1) < 64
    ma, mb_ = mb[0], mb[1]
    tail = jnp.where(low, ma[:, 128:256], pltpu.roll(mb_[:, 128:256], 64, 1))
    modul = jnp.concatenate([ma[:, 0:128], mb_[:, 0:128], tail], axis=1)
    for c in st_c:
        c.wait_recv()
    tot = st[0]
    for k in range(1, NZ):
        tot = tot + st[k]
    tot = jnp.transpose(jnp.concatenate([tot, jnp.zeros((120, 256), F32)], axis=0))
    average = tot[:, 0:1] / D
    variance = tot[:, 1:2] / D - average * average
    normed = (
        (ctx - average) * lax.rsqrt(variance + 1e-06) * (1.0 + modul[0:1]) + modul[1:2]
    ).astype(BF)
    for c in kx_core:
        c.wait_recv()
    for i in range(NX):
        for lo in (0, 1):
            rhs = jnp.concatenate(
                [jnp.concatenate([kx[i, c, lo, b] for b in range(3)], axis=1) for c in (0, 1)],
                axis=0,
            )
            part = lax.dot_general(
                normed, rhs, (((1,), (1,)), ((), ())), preferred_element_type=F32
            )
            at = (i * 2 + lo) * 384
            pt[:, :, at : at + 384] = part.reshape(NZ, 32, 384)

    steps = {}
    for way in (0, 1):
        to, half = (left, pl.ds(0, 16)) if way == 0 else (right, pl.ds(16, 16))
        for n in range(4):
            src, dst = rs_out.at[way, n], rs_in.at[way, n]
            if n == 0:
                src, dst = src.at[half], dst.at[half]
            steps[way, n] = net.copy(src, dst, to)

    def sum_step(n):
        for way in (0, 1):
            slot = 4 - n if way == 0 else 4 + n
            if n == 0:
                part = slice(0, 16) if way == 0 else slice(16, 32)
                rs_out[way, 0, part] = pt[at_z(slot), part].astype(BF)
            else:
                steps[way, n - 1].wait_recv()
                if n == 1:
                    part = slice(0, 16) if way == 0 else slice(16, 32)
                    rest = slice(16, 32) if way == 0 else slice(0, 16)
                    rs_out[way, 1, part] = (pt[at_z(slot), part] + rs_in[way, 0, part]).astype(BF)
                    rs_out[way, 1, rest] = pt[at_z(slot), rest].astype(BF)
                else:
                    rs_out[way, n] = (pt[at_z(slot)] + rs_in[way, n - 1]).astype(BF)
            steps[way, n].start()

    def stale_step(s):
        for r in stale:
            r.forward(s)

    sum_step(0)
    stale[2].forward(1)
    stale[3].forward(1)
    sum_step(1)
    stale[0].forward(2)
    stale[1].forward(2)
    sum_step(2)
    sum_step(3)
    stale[2].forward(2)
    stale[3].forward(2)
    steps[0, 3].wait_recv()
    steps[1, 3].wait_recv()
    tkv[...] = (pt[z] + rs_in[0, 3] + rs_in[1, 3]).astype(BF)
    t_opp = [
        net.copy(tkv.at[:, pl.ds(pl.multiple_of(o + theirs, 128), HALF)], b.at[0, 1], opposite)
        for o, b in ((0, tk), (D // 2, tv))
    ]
    for c in t_opp:
        c.start()
    tk[0, 0] = tkv[:, pl.ds(pl.multiple_of(mine, 128), HALF)]
    tv[0, 0] = tkv[:, pl.ds(pl.multiple_of(D // 2 + mine, 128), HALF)]
    tring = [
        Ring(net, lambda k, b=b, r=r: b.at[k, r], 32, left, right)
        for r in (0, 1)
        for b in (tk, tv)
    ]
    tring[0].start()
    tring[1].start()
    for c in t_opp:
        c.wait_recv()
    tring[2].start()
    tring[3].start()

    c2 = math.log2(math.e) / math.sqrt(HEAD)
    contract = (((1,), (1,)), ((), ()))

    def head(n):
        return pl.ds(pl.multiple_of(n * HEAD, HEAD), HEAD)

    def scores(q, k):
        return lax.dot_general(q, k, contract, preferred_element_type=F32) * c2

    for c in (c_q, c_fk, c_fv, c_sk, c_sv):
        c.wait()
    for c in qf_opp:
        c.wait_recv()

    def first_block(n, _):
        for r in (0, 1):
            k = jnp.concatenate([fk[r, :, head(n)], sk[0, 1 - r, :, head(n)]], axis=0)
            v = jnp.concatenate([fv[r, :, head(n)], sv[0, 1 - r, :, head(n)]], axis=0)
            s = scores(qb[r, :, head(n)], k)
            m = jnp.max(s, -1, keepdims=True)
            p = jnp.exp2(s - m)
            rows = pl.ds(r * 128, 128)
            mx[n, rows] = jnp.broadcast_to(m, (128, 128))
            dn[n, rows] = jnp.broadcast_to(jnp.sum(p, -1, keepdims=True), (128, 128))
            acc[n, rows] = jnp.dot(p.astype(BF), v, preferred_element_type=F32)
        return 0

    def attend(keys, values, mask=None):
        def body(n, _):
            q = qb[:, :, head(n)].reshape(256, HEAD)
            k = jnp.concatenate([b[..., head(n)].reshape(-1, HEAD) for b in keys], axis=0)
            v = jnp.concatenate([b[..., head(n)].reshape(-1, HEAD) for b in values], axis=0)
            s = scores(q, k)
            if mask is not None:
                s = jnp.where(mask, s, -jnp.inf)
            old = mx[n]
            m = jnp.maximum(old, jnp.max(s, -1, keepdims=True))
            p = jnp.exp2(s - m[:, 0:1])
            alpha = jnp.exp2(old - m)
            mx[n] = m
            dn[n] = dn[n] * alpha + jnp.sum(p, -1, keepdims=True)
            acc[n] = acc[n] * alpha + jnp.dot(p.astype(BF), v, preferred_element_type=F32)
            return 0

        lax.fori_loop(0, NH, body, 0)

    def attend_slots(*slots):
        attend([sk.at[k] for k in slots], [sv.at[k] for k in slots])

    def tring_step(s):
        for r in tring:
            r.forward(s)

    lax.fori_loop(0, NH, first_block, 0)
    tring_step(1)
    attend_slots(1, 7)
    tring_step(2)
    stale[0].forward(3)
    stale[1].forward(3)
    tring_step(3)
    stale[2].forward(3)
    stale[3].forward(3)
    attend_slots(2, 6)
    attend_slots(3, 5)
    for r in tring:
        r.finish()
    at = lax.broadcasted_iota(jnp.int32, (1, 512), 1)
    slot, rel, row = at // 64, (at // 32) % 2, at % 32
    position = at_z(slot) * 64 + jnp.where(rel == 0, h, 1 - h) * 32 + row
    attend([tk], [tv], position < len_ref[0])
    for r in stale:
        r.finish()
    attend_slots(4)

    def close(r, out):
        for n in range(NH):
            rows = pl.ds(r * 128, 128)
            out[:, n * HEAD : (n + 1) * HEAD] = (acc[n, rows] / dn[n, rows]).astype(BF)

    close(1, ob)
    o_c = net.copy(ob, ob_in, opposite)
    o_c.start()
    for n in range(NH):
        rows = pl.ds(0, 128)
        out_ref[0, :, head(h * NH + n)] = (acc[n, rows] / dn[n, rows]).astype(BF)
    o_c.wait_recv()
    out_ref[0, :, pl.ds(pl.multiple_of(theirs, 128), HALF)] = ob_in[...]
    net.drain()


N_COPIES = 160


def per_device(img_q, fresh_kv, stale_kv, text_states, ctx_weight, kv_weight, modulation, lengths):
    hbm = pl.BlockSpec(memory_space=pl.ANY)
    vmem = pl.BlockSpec(memory_space=pltpu.VMEM)
    smem = pl.BlockSpec(memory_space=pltpu.SMEM)
    return pl.pallas_call(
        kernel,
        out_shape=jax.ShapeDtypeStruct((1, 128, 1536), BF),
        in_specs=[hbm, hbm, hbm, hbm, vmem, vmem, vmem, smem],
        out_specs=vmem,
        scratch_shapes=[
            pltpu.VMEM((NZ, 32, 4096), BF),
            pltpu.VMEM((NY, 384, 128), BF),
            pltpu.VMEM((NY, 288, 128), BF),
            pltpu.VMEM((NX, 2, 2, 3, 256, 128), BF),
            pltpu.VMEM((NX, 2, 2, 3, 192, 128), BF),
            pltpu.VMEM((2, 8, 256), F32),
            pltpu.VMEM((NZ, 8, 256), F32),
            pltpu.VMEM((NZ, 32, D), F32),
            pltpu.VMEM((2, 4, 32, D), BF),
            pltpu.VMEM((2, 4, 32, D), BF),
            pltpu.VMEM((32, D), BF),
            pltpu.VMEM((NZ, 2, 32, HALF), BF),
            pltpu.VMEM((NZ, 2, 32, HALF), BF),
            pltpu.VMEM((NZ, 2, 128, HALF), BF),
            pltpu.VMEM((NZ, 2, 128, HALF), BF),
            pltpu.VMEM((2, 128, HALF), BF),
            pltpu.VMEM((2, 128, HALF), BF),
            pltpu.VMEM((2, 128, HALF), BF),
            pltpu.VMEM((NH, 256, HEAD), F32),
            pltpu.VMEM((NH, 256, HEAD), F32),
            pltpu.VMEM((NH, 256, HEAD), F32),
            pltpu.VMEM((128, HALF), BF),
            pltpu.VMEM((128, HALF), BF),
            pltpu.SemaphoreType.DMA((N_COPIES,)),
            pltpu.SemaphoreType.DMA((N_COPIES,)),
            pltpu.SemaphoreType.DMA((8,)),
        ],
        compiler_params=pltpu.CompilerParams(
            collective_id=0, has_side_effects=True, vmem_limit_bytes=50 << 20
        ),
    )(img_q, fresh_kv, stale_kv, text_states, ctx_weight, kv_weight, modulation, lengths)


def solution(mesh):
    in_specs = (
        P("img", "patch", None),
        P("img", "patch", None),
        P("img", "patch", None),
        P("img", "patch", None),
        P("img", "patch"),
        P("img", "patch"),
        P("img", None, "patch"),
        P("img"),
    )
    return jax.shard_map(
        per_device,
        mesh=mesh,
        in_specs=in_specs,
        out_specs=P("img", "patch", None),
        check_vma=False,
    )
```

time: 602 us -> 150 us (0.25)
  waiting for transfers between devices: 496 us -> 0 us
  Pallas kernels: 0 us -> 143 us
  blocking collectives: 38.6 us -> 0 us
  matrix products: 21.9 us -> 0 us
  local copies, waits for them, and re-layouts: 19.7 us -> 6 us
  between operations: 14 us -> 0.71 us
  other arithmetic: 10.9 us -> 0 us
    all_gather x4 -> x0, waiting for transfers between devices: 319 us -> none  [the longest x1 176 us: per_device(): key_block = lax.all_gather(stale_kv, 'patch', axis=1, tiled=True)[0]]
    psum x1 -> x0, waiting for transfers between devices: 175 us -> none  [per_device(): text_kv = lax.psum(partial_kv.astype(jnp.bfloat16), 'patch')]
    pallas_call x0 -> x1, Pallas kernels: none -> 143 us  [per_device(): pl.pallas_call(kernel, out_shape=jax.ShapeDtypeStruct((1, 128, 1536), BF)...]
    psum x1 -> x0, blocking collectives: 38.6 us -> none  [per_device(): lax.psum((jnp.sum(context, -1), jnp.sum(context * context, -1)), 'patch')]
    dot_general x6 -> x0, matrix products: 21.9 us -> none  [the longest x1 7.32 us: per_device(): jnp.einsum('rhn,nhd->rhd', block_weights.astype(jnp.bfloat16), block_valu...]
    slice x3 -> x0, local copies, waits for them, and re-layouts: 15.3 us -> none  [the longest x2 11.3 us: split_heads(): key_heads = kv_rows[:, :hd_width].reshape(count_rows, head_count, HEAD)]
  transfers between devices with their start and end apart: 5 -> 0, of which waited for: 4 -> 0; matrix products, arithmetic and copies ran while one was open for 3% -> 0% of each run, Pallas kernels for 0% -> 0%
where the time goes in v1:
time: 150 us
  Pallas kernels  143 us (95%)
  local copies, waits for them, and re-layouts  6 us (4%)
    pallas_call x1, Pallas kernels, per_device(): pl.pallas_call(kernel, out_shape=jax.ShapeDtypeStruct((1, 128, 1536), BF)...  143 us
    unnamed x14, local copies, waits for them, and re-layouts  6 us

profile of v1, /device:TPU:2, one launch (start us, length us, event | category | flops | bytes accessed | tf_op | source)
XLA Modules:
  0.0 149.8 jit_solution(10657065622262790412)
XLA Ops:
  0.7 0.0 copy-start.4
  0.7 0.0 copy-start.5
  0.7 1.0 copy.9.cw_ref
  1.7 0.0 copy-done.4
  1.7 0.0 copy-done.5
  1.7 0.0 copy-start
  1.7 1.1 copy-done
  2.9 0.0 copy-start.1
  2.9 1.1 copy-done.1
  4.0 0.0 copy-start.2
  4.0 1.0 copy-done.2
  5.0 0.0 copy-start.3
  5.0 0.9 copy-done.3
  5.9 143.1 %shard_map.82 = bf16[1,128,1536]{2,1,0:T(8,128)(2,1)S(1)} custom-call(bf16[1,128,1536]{2,1,0:T(8,128)(2,1)S(1)} %copy-done.2, bf16[1,128,3072]{2,1,0:T(8,128)(2,1)S(1)} %copy-done, bf16[1,128,3072]{2,1,0:T(8,128)(2,1)S(1)} %copy-done.1, bf16[1,32,4096]{2,1,0:T(8,128)(2,1)S(1)} %copy-done.3, bf16[256,192]{1,0:T(8,128)(2,1)S(1)} %copy.9.cw_ref, ...), custom_call_target="tpu_custom_call" | custom-call | tf_op jit(solution)/shard_map/pallas_call | solution.py:426
  149.0 0.7 copy.12
Async XLA Ops:
  0.7 1.1 copy-start.4
  0.7 1.1 copy-start.5
  1.7 1.1 copy-start
  2.9 1.1 copy-start.1
  4.0 1.0 copy-start.2
  5.0 0.9 copy-start.3

commit v2 on v0

v2 whole, which is shorter than its diff:
```python
import functools
import math

import jax
import jax.numpy as jnp
from jax import lax
from jax.experimental import pallas as pl
from jax.experimental.pallas import tpu as pltpu
from jax.sharding import PartitionSpec as P

D = 3072
HEAD = 128
NX, NY, NZ = 4, 4, 8
HALF = 768
NH = 6
MESH = pl.DeviceIdType.MESH
BF = jnp.bfloat16
F32 = jnp.float32


def device(x, y, z, core):
    return ((x * 2 + y % 2) * 2 + core, z * 2 + y // 2)


class Net:
    def __init__(self, send, recv):
        self.send, self.recv, self.used, self.copies = send, recv, 0, []

    def copy(self, src, dst, to):
        n = self.used
        self.used += 1
        c = pltpu.make_async_remote_copy(
            src_ref=src,
            dst_ref=dst,
            send_sem=self.send.at[n],
            recv_sem=self.recv.at[n],
            device_id=to,
            device_id_type=MESH,
        )
        self.copies.append(c)
        return c

    def drain(self):
        for c in self.copies:
            c.wait_send()


class Ring:
    def __init__(self, net, slot, far, left, right, first=None, by_origin=False):
        self.step = {}
        for s in range(4):
            for way in (far, 1 - far):
                if s == 3 and way != far:
                    continue
                a, b, to = (s, s + 1, right) if way == 0 else ((8 - s) % 8, 7 - s, left)
                src, dst = slot(a), slot(a if by_origin else b)
                if s == 0 and first is not None:
                    src = first
                self.step[s, way] = net.copy(src, dst, to)

    def start(self):
        for way in (0, 1):
            self.step[0, way].start()

    def forward(self, s):
        for way in (0, 1):
            self.step[s - 1, way].wait_recv()
            if (s, way) in self.step:
                self.step[s, way].start()

    def finish(self):
        for way in (0, 1):
            if (3, way) in self.step:
                self.step[3, way].wait_recv()


def kernel(
    q_hbm, fresh_hbm, stale_hbm, text_hbm, cw_hbm, kw_hbm, mod_hbm, len_ref, out_ref,
    tx, kraw, kpack, w0, w1, k0, k1, mraw, mb, st, pt, rs_out, rs_in, tkv, tk, tv, sk, sv, qb, fk, fv,
    acc, mx, dn, ob, ob_in, send_sem, recv_sem, loc_sem,
):
    img, patch = lax.axis_index("img"), lax.axis_index("patch")
    x, core = img // 4, img % 2
    z, h = patch // 2, patch % 2
    y = h * 2 + (img // 2) % 2
    right, left = device(x, y, (z + 1) % NZ, core), device(x, y, (z + 7) % NZ, core)
    zs = {k: device(x, y, (z + k) % NZ, core) for k in range(1, NZ)}
    xs = {k: device((x + k) % NX, y, z, core) for k in range(1, NX)}
    ys = {k: device(x, (y + k) % NY, z, core) for k in range(1, NY)}
    other = device(x, y, z, 1 - core)
    opposite = ys[2]
    mine, theirs = h * HALF, (1 - h) * HALF
    net = Net(send_sem, recv_sem)

    barrier = pltpu.get_barrier_semaphore()
    peers = [right, left, *xs.values(), *ys.values(), other]
    for d in peers:
        pl.semaphore_signal(barrier, inc=1, device_id=d, device_id_type=MESH)

    def at_z(k):
        return (z + NZ - k) % NZ

    def cols(ref, at):
        return ref.at[0, :, pl.ds(pl.multiple_of(at, 128), HALF)]

    locals_ = []

    def local(src, dst):
        c = pltpu.make_async_copy(src, dst, loc_sem.at[len(locals_)])
        locals_.append(c)
        c.start()
        return c

    def text_cols(p):
        return text_hbm.at[0, :, pl.ds(p * 2048, 2048)]

    c_kw = local(kw_hbm, kraw)
    c_mod = local(mod_hbm.at[0], mraw)
    cw = [cw_hbm.at[pl.ds(p * 96, 96)] for p in (0, 1)]
    c_cw = [local(cw[0], w0.at[x, core, y]), local(cw[1], w1.at[y, core, x])]
    c_text = [local(text_cols(p), tx.at[p, z]) for p in (0, 1)]
    c_img = [
        local(cols(q_hbm, mine), qb.at[0]),
        local(cols(fresh_hbm, mine), fk.at[0]),
        local(cols(fresh_hbm, D // 2 + mine), fv.at[0]),
        local(cols(stale_hbm, mine), sk.at[0, 0]),
        local(cols(stale_hbm, D // 2 + mine), sv.at[0, 0]),
    ]
    c_kw.wait()
    w = kraw[...]
    kpack[0:192] = w[:, 0:128]
    kpack[192:288] = jnp.concatenate([w[0:96, 128:192], w[96:192, 128:192]], axis=1)
    k0[x, core, y] = kpack[0:144]
    k1[y, core, x] = kpack[144:288]
    c_mod.wait()
    mb[h, 0:2, 0:192] = mraw[...]
    pl.semaphore_wait(barrier, len(peers))

    text = [Ring(net, lambda k, p=p: tx.at[p, at_z(k)], p, left, right, text_cols(p), True) for p in (0, 1)]

    class Spread:
        def __init__(self, buf, i, j, own, first, second):
            self.first = {k: net.copy(own, buf.at[i, core, j], first[k]) for k in first}
            self.second = {k: net.copy(buf.at[i, core], buf.at[i, core], second[k]) for k in second}
            self.core = {k: net.copy(buf.at[(i + 4 - k) % 4, core], buf.at[(i + 4 - k) % 4, core], other) for k in range(4)}

        def start(self):
            for c in self.first.values():
                c.start()

        def middle(self):
            for c in self.first.values():
                c.wait_recv()
            for k in (2, 1, 3):
                self.second[k].start()
            self.core[0].start()

        def pass_on(self):
            for k in (1, 3, 2):
                self.second[k].wait_recv()
                self.core[k].start()

        def finish(self):
            for c in self.core.values():
                c.wait_recv()

    ws = [Spread(w0, x, y, cw[0], ys, xs), Spread(w1, y, x, cw[1], xs, ys)]
    ks = [
        Spread(k0, x, y, kpack.at[pl.ds(0, 144)], ys, xs),
        Spread(k1, y, x, kpack.at[pl.ds(144, 144)], xs, ys),
    ]
    m_c = net.copy(mb.at[h], mb.at[h], opposite)
    s_opp = [
        net.copy(cols(stale_hbm, theirs), sk.at[0, 1], opposite),
        net.copy(cols(stale_hbm, D // 2 + theirs), sv.at[0, 1], opposite),
    ]
    qf_opp = [
        net.copy(cols(q_hbm, theirs), qb.at[1], opposite),
        net.copy(cols(fresh_hbm, theirs), fk.at[1], opposite),
        net.copy(cols(fresh_hbm, D // 2 + theirs), fv.at[1], opposite),
    ]
    stale = [
        Ring(net, lambda k, b=b, r=r: b.at[k, r], far, left, right, f)
        for r in (0, 1)
        for far, b, f in (
            (0, sk, cols(stale_hbm, mine) if r == 0 else None),
            (1, sv, cols(stale_hbm, D // 2 + mine) if r == 0 else None),
        )
    ]
    stale_work = []
    for s in range(4):
        for n, r in enumerate(stale):
            if s == 0:
                stale_work.append((r.start, s_opp[n - 2] if n >= 2 else None))
            else:
                stale_work.append((functools.partial(r.forward, s), None))

    def pump(n):
        for _ in range(min(n, len(stale_work))):
            go, before = stale_work.pop(0)
            if before is not None:
                before.wait_recv()
            go()

    def each(things, method, *args):
        for t in things:
            getattr(t, method)(*args)

    def tile(a, b, i, c, lo):
        return [jnp.concatenate([a[i, c, t], b[t, c, i]], axis=0) for t in (lo, 2 + lo)]

    held = {}

    def context():
        each(c_text, "wait")
        ctx = jnp.zeros((256, 384), F32)
        for i in range(NX):
            blocks = []
            for lo in (0, 1):
                for c in (0, 1):
                    a, b = tile(w0, w1, i, c, lo)
                    blocks.append(jnp.concatenate([a[0:128], b[0:128], a[128:], b[128:]], axis=0))
            rhs = jnp.concatenate(blocks, axis=1)
            lhs = tx[i // 2, :, :, (i % 2) * 1024 : (i % 2 + 1) * 1024].reshape(256, 1024)
            ctx = ctx + lax.dot_general(
                lhs, rhs, (((1,), (1,)), ((), ())), preferred_element_type=F32
            )
        lane = lax.broadcasted_iota(jnp.int32, (256, 128), 1)
        s1 = jnp.sum(ctx, -1, keepdims=True)
        s2 = jnp.sum(ctx * ctx, -1, keepdims=True)
        both = jnp.where(lane == 0, s1, jnp.where(lane == 1, s2, 0.0))
        st[0] = jnp.transpose(both)[0:8]
        st_c = [net.copy(st.at[0], st.at[k], zs[k]) for k in zs]
        for c in st_c:
            c.start()
        held.update(ctx=ctx, st_c=st_c)

    def norm():
        ctx, st_c = held["ctx"], held["st_c"]
        m_c.wait_recv()
        low = lax.broadcasted_iota(jnp.int32, (8, 128), 1) < 64
        ma, mb_ = mb[0], mb[1]
        tail = jnp.where(low, ma[:, 128:256], pltpu.roll(mb_[:, 128:256], 64, 1))
        modul = jnp.concatenate([ma[:, 0:128], mb_[:, 0:128], tail], axis=1)
        for c in st_c:
            c.wait_recv()
        tot = st[0]
        for k in range(1, NZ):
            tot = tot + st[k]
        tot = jnp.transpose(jnp.concatenate([tot, jnp.zeros((120, 256), F32)], axis=0))
        average = tot[:, 0:1] / D
        variance = tot[:, 1:2] / D - average * average
        normed = (
            (ctx - average) * lax.rsqrt(variance + 1e-06) * (1.0 + modul[0:1]) + modul[1:2]
        ).astype(BF)
        held["normed"] = normed

    def partial_kv():
        normed = held["normed"]
        for i in range(NX):
            for lo in (0, 1):
                blocks = []
                for c in (0, 1):
                    a, b = tile(k0, k1, i, c, lo)
                    ra, rb = a[192:], b[192:]
                    last = jnp.concatenate(
                        [
                            jnp.concatenate([ra[:, 0:64], rb[:, 0:64]], axis=1),
                            jnp.concatenate([ra[:, 64:], rb[:, 64:]], axis=1),
                        ],
                        axis=0,
                    )
                    blocks.append(jnp.concatenate([a[0:192], b[0:192], last], axis=1))
                part = lax.dot_general(
                    normed,
                    jnp.concatenate(blocks, axis=0),
                    (((1,), (1,)), ((), ())),
                    preferred_element_type=F32,
                )
                at = (i * 2 + lo) * 384
                pt[:, :, at : at + 384] = part.reshape(NZ, 32, 384)

    parts = (slice(0, D // 2), slice(D // 2, D))
    steps = {}
    for n in range(4):
        for way in (0, 1):
            for p in (way, 1 - way):
                if n > 0 or p == way:
                    to = left if way == 0 else right
                    steps[n, way, p] = net.copy(rs_out.at[way, n, p], rs_in.at[way, n, p], to)

    def sum_step(n):
        for p in (0, 1):
            for way in (0, 1):
                if (n, way, p) not in steps:
                    continue
                term = pt[at_z(4 - n if way == 0 else 4 + n), :, parts[p]]
                if (n - 1, way, p) in steps:
                    steps[n - 1, way, p].wait_recv()
                    term = term + rs_in[way, n - 1, p]
                rs_out[way, n, p] = term.astype(BF)
                steps[n, way, p].start()

    tring = [
        Ring(net, lambda k, b=b, r=r: b.at[k, r], far, left, right)
        for r in (0, 1)
        for far, b in ((0, tk), (1, tv))
    ]
    t_opp = []

    def sum_end():
        for p, b in ((0, tk), (1, tv)):
            for way in (0, 1):
                steps[3, way, p].wait_recv()
            tkv[p] = (pt[z, :, parts[p]] + rs_in[0, 3, p] + rs_in[1, 3, p]).astype(BF)
            c = net.copy(tkv.at[p, :, pl.ds(pl.multiple_of(theirs, 128), HALF)], b.at[0, 1], opposite)
            c.start()
            t_opp.append(c)
            b[0, 0] = tkv[p, :, pl.ds(pl.multiple_of(mine, 128), HALF)]
            tring[p].start()

    def ring_opposite():
        for p in (0, 1):
            t_opp[p].wait_recv()
            tring[2 + p].start()

    c2 = math.log2(math.e) / math.sqrt(HEAD)
    contract = (((1,), (1,)), ((), ()))

    def head(n):
        return pl.ds(pl.multiple_of(n * HEAD, HEAD), HEAD)

    def scores(q, k):
        return lax.dot_general(q, k, contract, preferred_element_type=F32) * c2

    def first_block(n, _):
        for r in (0, 1):
            k = jnp.concatenate([fk[r, :, head(n)], sk[0, 1 - r, :, head(n)]], axis=0)
            v = jnp.concatenate([fv[r, :, head(n)], sv[0, 1 - r, :, head(n)]], axis=0)
            s = scores(qb[r, :, head(n)], k)
            m = jnp.max(s, -1, keepdims=True)
            p = jnp.exp2(s - m)
            rows = pl.ds(r * 128, 128)
            mx[n, rows] = jnp.broadcast_to(m, (128, 128))
            dn[n, rows] = jnp.broadcast_to(jnp.sum(p, -1, keepdims=True), (128, 128))
            acc[n, rows] = jnp.dot(p.astype(BF), v, preferred_element_type=F32)
        return 0

    def attend(keys, values, mask=None, block=None, heads=(0, NH)):
        rows = slice(None) if block is None else pl.ds(block * 128, 128)

        def body(n, _):
            if block is None:
                q = qb[:, :, head(n)].reshape(256, HEAD)
            else:
                q = qb[block, :, head(n)]
            k = jnp.concatenate([b[..., head(n)].reshape(-1, HEAD) for b in keys], axis=0)
            v = jnp.concatenate([b[..., head(n)].reshape(-1, HEAD) for b in values], axis=0)
            s = scores(q, k)
            if mask is not None:
                s = jnp.where(mask, s, -jnp.inf)
            old = mx[n, rows]
            m = jnp.maximum(old, jnp.max(s, -1, keepdims=True))
            p = jnp.exp2(s - m[:, 0:1])
            alpha = jnp.exp2(old - m)
            mx[n, rows] = m
            dn[n, rows] = dn[n, rows] * alpha + jnp.sum(p, -1, keepdims=True)
            acc[n, rows] = acc[n, rows] * alpha + jnp.dot(
                p.astype(BF), v, preferred_element_type=F32
            )
            return 0

        lax.fori_loop(*heads, body, 0)

    def attend_slots(*slots):
        attend([sk.at[k] for k in slots], [sv.at[k] for k in slots])

    def first():
        each(c_img, "wait")
        each(qf_opp, "wait_recv")
        lax.fori_loop(0, NH, first_block, 0)

    def attend_text(*slots):
        n = len(slots) * 64
        at = lax.broadcasted_iota(jnp.int32, (1, n), 1)
        slot = jnp.full((1, n), slots[0], jnp.int32)
        for k in range(1, len(slots)):
            slot = jnp.where(at >= k * 64, slots[k], slot)
        position = at_z(slot) * 64 + jnp.where((at // 32) % 2 == 0, h, 1 - h) * 32 + at % 32
        attend([tk.at[k] for k in slots], [tv.at[k] for k in slots], position < len_ref[0])

    ops = {
        "wf": lambda: each(ws, "finish"),
        "wp": lambda: each(ws, "pass_on"),
        "ws": lambda: each(ws, "start"),
        "wm": lambda: (each(c_cw, "wait"), each(ws, "middle")),
        "ks": lambda: each(ks, "start"),
        "km": lambda: each(ks, "middle"),
        "kp": lambda: each(ks, "pass_on"),
        "kf": lambda: each(ks, "finish"),
        "ms": m_c.start,
        "so": lambda: each(s_opp, "start"),
        "qf": lambda: each(qf_opp, "start"),
        "T1": context,
        "NO": norm,
        "T2": partial_kv,
        "rf": sum_end,
        "to": ring_opposite,
        "P": lambda: pump(1),
        "PP": lambda: pump(2),
        "PA": lambda: pump(16),
        "sf": lambda: each(stale, "finish"),
        "A0": first,
        "ts": lambda: each(text, "start"),
        "tf": lambda: each(text, "finish"),
        "af": lambda: each(tring, "finish"),
    }
    for n in range(4):
        ops[f"r{n}"] = functools.partial(sum_step, n)
        ops[f"t{n}"] = functools.partial(each, text, "forward", n)
        ops[f"a{n}"] = functools.partial(each, tring, "forward", n)
        ops[f"b{n}"] = functools.partial(each, tring[0:2], "forward", n)
        ops[f"c{n}"] = functools.partial(each, tring[2:4], "forward", n)
    for op in PLAN:
        if op in ops:
            ops[op]()
        elif op[0] == "S":
            attend_slots(*map(int, op[1:]))
        else:
            attend_text(*map(int, op[1:]))

    o_c = [net.copy(ob.at[p], ob_in.at[p], opposite) for p in (0, 1)]
    last = [sk.at[4]], [sv.at[4]]
    for p in (0, 1):
        attend(*last, block=1, heads=(3 * p, 3 * p + 3))
        for n in range(3):
            part = acc[3 * p + n, 128:256] / dn[3 * p + n, 128:256]
            ob[p, :, n * HEAD : (n + 1) * HEAD] = part.astype(BF)
        o_c[p].start()
    attend(*last, block=0)
    for n in range(NH):
        out_ref[0, :, head(h * NH + n)] = (acc[n, 0:128] / dn[n, 0:128]).astype(BF)
    for p in (0, 1):
        o_c[p].wait_recv()
        at = pl.multiple_of(theirs + p * HALF // 2, 128)
        out_ref[0, :, pl.ds(at, HALF // 2)] = ob_in[p]
    net.drain()


N_COPIES = 192
PLAN = (
    "ts", "ws", "ms", "ks", "wm", "so", "t1", "t2", "P", "P", "wp", "km",
    "t3", "P", "wf", "tf", "P", "T1", "kp", "qf", "P", "P", "NO", "kf",
    "T2", "r0", "P", "r1", "P", "A0", "r2", "P", "r3", "P", "rf", "P",
    "to", "S17", "a1", "P", "X017", "a2", "P", "S26", "X26", "a3", "P", "X35",
    "PA", "S35", "af", "X4", "sf",
)


def per_device(img_q, fresh_kv, stale_kv, text_states, ctx_weight, kv_weight, modulation, lengths):
    hbm = pl.BlockSpec(memory_space=pltpu.HBM)
    vmem = pl.BlockSpec(memory_space=pltpu.VMEM)
    smem = pl.BlockSpec(memory_space=pltpu.SMEM)
    return pl.pallas_call(
        kernel,
        out_shape=jax.ShapeDtypeStruct((1, 128, 1536), BF),
        in_specs=[hbm] * 7 + [smem],
        out_specs=vmem,
        scratch_shapes=[
            pltpu.VMEM((2, NZ, 32, 2048), BF),
            pltpu.VMEM((192, 192), BF),
            pltpu.VMEM((288, 128), BF),
            pltpu.VMEM((NX, 2, NY, 96, 256), BF),
            pltpu.VMEM((NY, 2, NX, 96, 256), BF),
            pltpu.VMEM((NX, 2, NY, 144, 128), BF),
            pltpu.VMEM((NY, 2, NX, 144, 128), BF),
            pltpu.VMEM((2, 192), F32),
            pltpu.VMEM((2, 8, 256), F32),
            pltpu.VMEM((NZ, 8, 256), F32),
            pltpu.VMEM((NZ, 32, D), F32),
            pltpu.VMEM((2, 4, 2, 32, D // 2), BF),
            pltpu.VMEM((2, 4, 2, 32, D // 2), BF),
            pltpu.VMEM((2, 32, D // 2), BF),
            pltpu.VMEM((NZ, 2, 32, HALF), BF),
            pltpu.VMEM((NZ, 2, 32, HALF), BF),
            pltpu.VMEM((NZ, 2, 128, HALF), BF),
            pltpu.VMEM((NZ, 2, 128, HALF), BF),
            pltpu.VMEM((2, 128, HALF), BF),
            pltpu.VMEM((2, 128, HALF), BF),
            pltpu.VMEM((2, 128, HALF), BF),
            pltpu.VMEM((NH, 256, HEAD), F32),
            pltpu.VMEM((NH, 256, HEAD), F32),
            pltpu.VMEM((NH, 256, HEAD), F32),
            pltpu.VMEM((2, 128, HALF // 2), BF),
            pltpu.VMEM((2, 128, HALF // 2), BF),
            pltpu.SemaphoreType.DMA((N_COPIES,)),
            pltpu.SemaphoreType.DMA((N_COPIES,)),
            pltpu.SemaphoreType.DMA((16,)),
        ],
        compiler_params=pltpu.CompilerParams(
            collective_id=0, has_side_effects=True, vmem_limit_bytes=60 << 20
        ),
    )(img_q, fresh_kv, stale_kv, text_states, ctx_weight.T, kv_weight, modulation, lengths)


def solution(mesh):
    in_specs = (
        P("img", "patch", None),
        P("img", "patch", None),
        P("img", "patch", None),
        P("img", "patch", None),
        P("img", "patch"),
        P("img", "patch"),
        P("img", None, "patch"),
        P("img"),
    )
    return jax.shard_map(
        per_device,
        mesh=mesh,
        in_specs=in_specs,
        out_specs=P("img", "patch", None),
        check_vma=False,
    )
```

time: 602 us -> 135 us (0.22)
  waiting for transfers between devices: 496 us -> 0 us
  Pallas kernels: 0 us -> 132 us
  blocking collectives: 38.6 us -> 0 us
  matrix products: 21.9 us -> 0 us
  local copies, waits for them, and re-layouts: 19.7 us -> 1.77 us
  between operations: 14 us -> 0.66 us
  other arithmetic: 10.9 us -> 0 us
    all_gather x4 -> x0, waiting for transfers between devices: 319 us -> none  [the longest x1 176 us: per_device(): key_block = lax.all_gather(stale_kv, 'patch', axis=1, tiled=True)[0]]
    psum x1 -> x0, waiting for transfers between devices: 175 us -> none  [per_device(): text_kv = lax.psum(partial_kv.astype(jnp.bfloat16), 'patch')]
    pallas_call x0 -> x1, Pallas kernels: none -> 132 us  [per_device(): pl.pallas_call(kernel, out_shape=jax.ShapeDtypeStruct((1, 128, 1536), BF)...]
    psum x1 -> x0, blocking collectives: 38.6 us -> none  [per_device(): lax.psum((jnp.sum(context, -1), jnp.sum(context * context, -1)), 'patch')]
    dot_general x6 -> x0, matrix products: 21.9 us -> none  [the longest x1 7.32 us: per_device(): jnp.einsum('rhn,nhd->rhd', block_weights.astype(jnp.bfloat16), block_valu...]
    slice x3 -> x0, local copies, waits for them, and re-layouts: 15.3 us -> none  [the longest x2 11.3 us: split_heads(): key_heads = kv_rows[:, :hd_width].reshape(count_rows, head_count, HEAD)]
  transfers between devices with their start and end apart: 5 -> 0, of which waited for: 4 -> 0; matrix products, arithmetic and copies ran while one was open for 3% -> 0% of each run, Pallas kernels for 0% -> 0%
where the time goes in v2:
time: 135 us; the launch traced here: 134 us
  Pallas kernels  132 us (98%)
  local copies, waits for them, and re-layouts  1.77 us (1%)
    pallas_call x1, Pallas kernels, per_device(): pl.pallas_call(kernel, out_shape=jax.ShapeDtypeStruct((1, 128, 1536), BF)...  132 us

profile of v2, /device:TPU:2, one launch (start us, length us, event | category | flops | bytes accessed | tf_op | source)
XLA Modules:
  0.0 134.3 jit_solution(13019024636651615636)
XLA Ops:
  0.7 131.9 %shard_map.82 = bf16[1,128,1536]{2,1,0:T(8,128)(2,1)} custom-call(bf16[1,128,1536]{2,1,0:T(8,128)(2,1)} %q_hbm.1, bf16[1,128,3072]{2,1,0:T(8,128)(2,1)} %fresh_hbm.1, bf16[1,128,3072]{2,1,0:T(8,128)(2,1)} %stale_hbm.1, bf16[1,32,4096]{2,1,0:T(8,128)(2,1)} %text_hbm.1, bf16[192,256]{1,0:T(8,128)(2,1)} %bitcast.1, bf16[192,192]{1,0:T(8,128)(2,1)} %kw_hbm.1, ...), custom_call_target="tpu_custom_call" | custom-call | tf_op jit(solution)/shard_map/pallas_call | solution.py:464
  132.6 1.8 %copy.11 = bf16[1,128,1536]{2,1,0:T(8,128)(2,1)} copy(bf16[1,128,1536]{2,1,0:T(8,128)(2,1)} %shard_map.82) | data formatting | bytes 786432

commit v3 on v2

--- a/solution.py
+++ b/solution.py
@@ -12,6 +12,7 @@
 HEAD = 128
 NX, NY, NZ = 4, 4, 8
 HALF = 768
+GROUP = 384
 NH = 6
 MESH = pl.DeviceIdType.MESH
 BF = jnp.bfloat16
@@ -75,9 +76,9 @@
 
 
 def kernel(
-    q_hbm, fresh_hbm, stale_hbm, text_hbm, cw_hbm, kw_hbm, mod_hbm, len_ref, out_ref,
+    q_hbm, fresh_hbm, stale_hbm, text_hbm, cw_hbm, kw_hbm, mod_hbm, len_ref, out_hbm,
     tx, kraw, kpack, w0, w1, k0, k1, mraw, mb, st, pt, rs_out, rs_in, tkv, tk, tv, sk, sv, qb, fk, fv,
-    acc, mx, dn, ob, ob_in, send_sem, recv_sem, loc_sem,
+    acc, mx, dn, ob, send_sem, recv_sem, loc_sem,
 ):
     img, patch = lax.axis_index("img"), lax.axis_index("patch")
     x, core = img // 4, img % 2
@@ -100,8 +101,11 @@
     def at_z(k):
         return (z + NZ - k) % NZ
 
-    def cols(ref, at):
-        return ref.at[0, :, pl.ds(pl.multiple_of(at, 128), HALF)]
+    def cols(ref, at, width=HALF):
+        return ref.at[0, :, pl.ds(pl.multiple_of(at, 128), width)]
+
+    def group(at, g, value):
+        return cols(stale_hbm, (D // 2 if value else 0) + at + g * GROUP, GROUP)
 
     locals_ = []
 
@@ -123,8 +127,8 @@
         local(cols(q_hbm, mine), qb.at[0]),
         local(cols(fresh_hbm, mine), fk.at[0]),
         local(cols(fresh_hbm, D // 2 + mine), fv.at[0]),
-        local(cols(stale_hbm, mine), sk.at[0, 0]),
-        local(cols(stale_hbm, D // 2 + mine), sv.at[0, 0]),
+        *(local(group(mine, g, 0), sk.at[g, 0, 0]) for g in (0, 1)),
+        *(local(group(mine, g, 1), sv.at[g, 0, 0]) for g in (0, 1)),
     ]
     c_kw.wait()
     w = kraw[...]
@@ -170,37 +174,37 @@
         Spread(k1, y, x, kpack.at[pl.ds(144, 144)], xs, ys),
     ]
     m_c = net.copy(mb.at[h], mb.at[h], opposite)
-    s_opp = [
-        net.copy(cols(stale_hbm, theirs), sk.at[0, 1], opposite),
-        net.copy(cols(stale_hbm, D // 2 + theirs), sv.at[0, 1], opposite),
-    ]
+    s_opp = {
+        (g, v): net.copy(group(theirs, g, v), b.at[g, 0, 1], opposite)
+        for g in (0, 1)
+        for v, b in ((0, sk), (1, sv))
+    }
     qf_opp = [
         net.copy(cols(q_hbm, theirs), qb.at[1], opposite),
         net.copy(cols(fresh_hbm, theirs), fk.at[1], opposite),
         net.copy(cols(fresh_hbm, D // 2 + theirs), fv.at[1], opposite),
     ]
-    stale = [
-        Ring(net, lambda k, b=b, r=r: b.at[k, r], far, left, right, f)
+    stale = {
+        (r, g, v): Ring(
+            net, lambda k, b=b, r=r, g=g: b.at[g, k, r], v, left, right,
+            None if r else group(mine, g, v),
+        )
         for r in (0, 1)
-        for far, b, f in (
-            (0, sk, cols(stale_hbm, mine) if r == 0 else None),
-            (1, sv, cols(stale_hbm, D // 2 + mine) if r == 0 else None),
-        )
-    ]
-    stale_work = []
-    for s in range(4):
-        for n, r in enumerate(stale):
-            if s == 0:
-                stale_work.append((r.start, s_opp[n - 2] if n >= 2 else None))
-            else:
-                stale_work.append((functools.partial(r.forward, s), None))
+        for g in (0, 1)
+        for v, b in ((0, sk), (1, sv))
+    }
+    stale_work = list(STALE)
 
     def pump(n):
-        for _ in range(min(n, len(stale_work))):
-            go, before = stale_work.pop(0)
-            if before is not None:
-                before.wait_recv()
-            go()
+        for _ in range(n):
+            s, r, g = stale_work.pop(0)
+            for v in (0, 1):
+                if s > 0:
+                    stale[r, g, v].forward(s)
+                else:
+                    if r == 1:
+                        s_opp[g, v].wait_recv()
+                    stale[r, g, v].start()
 
     def each(things, method, *args):
         for t in things:
@@ -328,15 +332,16 @@
     contract = (((1,), (1,)), ((), ()))
 
     def head(n):
-        return pl.ds(pl.multiple_of(n * HEAD, HEAD), HEAD)
+        return pl.ds(n * HEAD, HEAD)
 
     def scores(q, k):
         return lax.dot_general(q, k, contract, preferred_element_type=F32) * c2
 
-    def first_block(n, _):
+    def first_block(g, n):
         for r in (0, 1):
-            k = jnp.concatenate([fk[r, :, head(n)], sk[0, 1 - r, :, head(n)]], axis=0)
-            v = jnp.concatenate([fv[r, :, head(n)], sv[0, 1 - r, :, head(n)]], axis=0)
+            at = head(n - 3 * g)
+            k = jnp.concatenate([fk[r, :, head(n)], sk[g, 0, 1 - r, :, at]], axis=0)
+            v = jnp.concatenate([fv[r, :, head(n)], sv[g, 0, 1 - r, :, at]], axis=0)
             s = scores(qb[r, :, head(n)], k)
             m = jnp.max(s, -1, keepdims=True)
             p = jnp.exp2(s - m)
@@ -344,18 +349,18 @@
             mx[n, rows] = jnp.broadcast_to(m, (128, 128))
             dn[n, rows] = jnp.broadcast_to(jnp.sum(p, -1, keepdims=True), (128, 128))
             acc[n, rows] = jnp.dot(p.astype(BF), v, preferred_element_type=F32)
-        return 0
 
     def attend(keys, values, mask=None, block=None, heads=(0, NH)):
+        first = heads[0]
         rows = slice(None) if block is None else pl.ds(block * 128, 128)
 
-        def body(n, _):
+        def body(n):
             if block is None:
                 q = qb[:, :, head(n)].reshape(256, HEAD)
             else:
                 q = qb[block, :, head(n)]
-            k = jnp.concatenate([b[..., head(n)].reshape(-1, HEAD) for b in keys], axis=0)
-            v = jnp.concatenate([b[..., head(n)].reshape(-1, HEAD) for b in values], axis=0)
+            k = jnp.concatenate([b[..., head(n - first)].reshape(-1, HEAD) for b in keys], axis=0)
+            v = jnp.concatenate([b[..., head(n - first)].reshape(-1, HEAD) for b in values], axis=0)
             s = scores(q, k)
             if mask is not None:
                 s = jnp.where(mask, s, -jnp.inf)
@@ -368,17 +373,24 @@
             acc[n, rows] = acc[n, rows] * alpha + jnp.dot(
                 p.astype(BF), v, preferred_element_type=F32
             )
-            return 0
-
-        lax.fori_loop(*heads, body, 0)
-
-    def attend_slots(*slots):
-        attend([sk.at[k] for k in slots], [sv.at[k] for k in slots])
+
+        for n in range(*heads):
+            body(n)
+
+    def attend_slots(g, *slots, block=None):
+        attend(
+            [sk.at[g, k] for k in slots],
+            [sv.at[g, k] for k in slots],
+            block=block,
+            heads=(3 * g, 3 * g + 3),
+        )
 
     def first():
         each(c_img, "wait")
         each(qf_opp, "wait_recv")
-        lax.fori_loop(0, NH, first_block, 0)
+        for g in (0, 1):
+            for n in range(3 * g, 3 * g + 3):
+                first_block(g, n)
 
     def attend_text(*slots):
         n = len(slots) * 64
@@ -388,6 +400,27 @@
             slot = jnp.where(at >= k * 64, slots[k], slot)
         position = at_z(slot) * 64 + jnp.where((at // 32) % 2 == 0, h, 1 - h) * 32 + at % 32
         attend([tk.at[k] for k in slots], [tv.at[k] for k in slots], position < len_ref[0])
+
+    def out_cols(g):
+        return cols(out_hbm, mine + g * GROUP, GROUP)
+
+    o_c = [net.copy(ob.at[1, g], out_cols(g), opposite) for g in (0, 1)]
+    own = []
+
+    def finish(g):
+        for r in (0, 1):
+            for v in (0, 1):
+                stale[r, g, v].finish()
+        for block in (1, 0):
+            attend_slots(g, 4, block=block)
+            rows = pl.ds(block * 128, 128)
+            for n in range(3):
+                part = acc[3 * g + n, rows] / dn[3 * g + n, rows]
+                ob[block, g, :, n * HEAD : (n + 1) * HEAD] = part.astype(BF)
+            if block == 1:
+                o_c[g].start()
+            else:
+                own.append(local(ob.at[0, g], out_cols(g)))
 
     ops = {
         "wf": lambda: each(ws, "finish"),
@@ -399,7 +432,7 @@
         "kp": lambda: each(ks, "pass_on"),
         "kf": lambda: each(ks, "finish"),
         "ms": m_c.start,
-        "so": lambda: each(s_opp, "start"),
+        "so": lambda: each(s_opp.values(), "start"),
         "qf": lambda: each(qf_opp, "start"),
         "T1": context,
         "NO": norm,
@@ -407,9 +440,9 @@
         "rf": sum_end,
         "to": ring_opposite,
         "P": lambda: pump(1),
-        "PP": lambda: pump(2),
-        "PA": lambda: pump(16),
-        "sf": lambda: each(stale, "finish"),
+        "PA": lambda: pump(len(stale_work)),
+        "F0": lambda: finish(0),
+        "F1": lambda: finish(1),
         "A0": first,
         "ts": lambda: each(text, "start"),
         "tf": lambda: each(text, "finish"),
@@ -425,47 +458,40 @@
         if op in ops:
             ops[op]()
         elif op[0] == "S":
-            attend_slots(*map(int, op[1:]))
+            attend_slots(0, *map(int, op[1:]))
+            attend_slots(1, *map(int, op[1:]))
+        elif op[0] in "DE":
+            attend_slots("DE".index(op[0]), *map(int, op[1:]))
         else:
             attend_text(*map(int, op[1:]))
 
-    o_c = [net.copy(ob.at[p], ob_in.at[p], opposite) for p in (0, 1)]
-    last = [sk.at[4]], [sv.at[4]]
-    for p in (0, 1):
-        attend(*last, block=1, heads=(3 * p, 3 * p + 3))
-        for n in range(3):
-            part = acc[3 * p + n, 128:256] / dn[3 * p + n, 128:256]
-            ob[p, :, n * HEAD : (n + 1) * HEAD] = part.astype(BF)
-        o_c[p].start()
-    attend(*last, block=0)
-    for n in range(NH):
-        out_ref[0, :, head(h * NH + n)] = (acc[n, 0:128] / dn[n, 0:128]).astype(BF)
-    for p in (0, 1):
-        o_c[p].wait_recv()
-        at = pl.multiple_of(theirs + p * HALF // 2, 128)
-        out_ref[0, :, pl.ds(at, HALF // 2)] = ob_in[p]
+    each(own, "wait")
+    each(o_c, "wait_recv")
     net.drain()
 
 
-N_COPIES = 192
+N_COPIES = 224
+STALE = (
+    *((0, r, g) for r in (0, 1) for g in (0, 1)),
+    *((s, r, g) for s in (1, 2, 3) for g in (0, 1) for r in (0, 1)),
+)
 PLAN = (
-    "ts", "ws", "ms", "ks", "wm", "so", "t1", "t2", "P", "P", "wp", "km",
-    "t3", "P", "wf", "tf", "P", "T1", "kp", "qf", "P", "P", "NO", "kf",
+    "ts", "ws", "ms", "wm", "ks", "so", "t1", "t2", "P", "P", "t3", "wp",
+    "km", "P", "P", "wf", "tf", "T1", "kp", "qf", "P", "P", "NO", "kf",
     "T2", "r0", "P", "r1", "P", "A0", "r2", "P", "r3", "P", "rf", "P",
-    "to", "S17", "a1", "P", "X017", "a2", "P", "S26", "X26", "a3", "P", "X35",
-    "PA", "S35", "af", "X4", "sf",
+    "to", "S17", "a1", "P", "X017", "a2", "P", "S26", "X26", "a3", "P", "PA",
+    "S35", "af", "X354", "F0", "F1",
 )
 
 
 def per_device(img_q, fresh_kv, stale_kv, text_states, ctx_weight, kv_weight, modulation, lengths):
     hbm = pl.BlockSpec(memory_space=pltpu.HBM)
-    vmem = pl.BlockSpec(memory_space=pltpu.VMEM)
     smem = pl.BlockSpec(memory_space=pltpu.SMEM)
     return pl.pallas_call(
         kernel,
         out_shape=jax.ShapeDtypeStruct((1, 128, 1536), BF),
         in_specs=[hbm] * 7 + [smem],
-        out_specs=vmem,
+        out_specs=hbm,
         scratch_shapes=[
             pltpu.VMEM((2, NZ, 32, 2048), BF),
             pltpu.VMEM((192, 192), BF),
@@ -483,22 +509,21 @@
             pltpu.VMEM((2, 32, D // 2), BF),
             pltpu.VMEM((NZ, 2, 32, HALF), BF),
             pltpu.VMEM((NZ, 2, 32, HALF), BF),
-            pltpu.VMEM((NZ, 2, 128, HALF), BF),
-            pltpu.VMEM((NZ, 2, 128, HALF), BF),
+            pltpu.VMEM((2, NZ, 2, 128, GROUP), BF),
+            pltpu.VMEM((2, NZ, 2, 128, GROUP), BF),
             pltpu.VMEM((2, 128, HALF), BF),
             pltpu.VMEM((2, 128, HALF), BF),
             pltpu.VMEM((2, 128, HALF), BF),
             pltpu.VMEM((NH, 256, HEAD), F32),
             pltpu.VMEM((NH, 256, HEAD), F32),
             pltpu.VMEM((NH, 256, HEAD), F32),
-            pltpu.VMEM((2, 128, HALF // 2), BF),
-            pltpu.VMEM((2, 128, HALF // 2), BF),
+            pltpu.VMEM((2, 2, 128, HALF // 2), BF),
             pltpu.SemaphoreType.DMA((N_COPIES,)),
             pltpu.SemaphoreType.DMA((N_COPIES,)),
-            pltpu.SemaphoreType.DMA((16,)),
+            pltpu.SemaphoreType.DMA((24,)),
         ],
         compiler_params=pltpu.CompilerParams(
-            collective_id=0, has_side_effects=True, vmem_limit_bytes=60 << 20
+            collective_id=0, has_side_effects=True, vmem_limit_bytes=58 << 20
         ),
     )(img_q, fresh_kv, stale_kv, text_states, ctx_weight.T, kv_weight, modulation, lengths)
 

time: 135 us -> 132 us (0.978)
  Pallas kernels: 132 us -> 129 us
    pallas_call x1, Pallas kernels: 132 us -> 129 us  [per_device(): pl.pallas_call(kernel, out_shape=jax.ShapeDtypeStruct((1, 128, 1536), BF)...]
where the time goes in v3:
time: 132 us
  Pallas kernels  129 us (98%)
  local copies, waits for them, and re-layouts  1.77 us (1%)
    pallas_call x1, Pallas kernels, per_device(): pl.pallas_call(kernel, out_shape=jax.ShapeDtypeStruct((1, 128, 1536), BF)...  129 us

profile of v3, /device:TPU:2, one launch (start us, length us, event | category | flops | bytes accessed | tf_op | source)
XLA Modules:
  0.0 131.9 jit_solution(3785848295677316917)
XLA Ops:
  0.7 129.5 %shard_map.82 = bf16[1,128,1536]{2,1,0:T(8,128)(2,1)} custom-call(bf16[1,128,1536]{2,1,0:T(8,128)(2,1)} %q_hbm.1, bf16[1,128,3072]{2,1,0:T(8,128)(2,1)} %fresh_hbm.1, bf16[1,128,3072]{2,1,0:T(8,128)(2,1)} %stale_hbm.1, bf16[1,32,4096]{2,1,0:T(8,128)(2,1)} %text_hbm.1, bf16[192,256]{1,0:T(8,128)(2,1)} %bitcast.1, bf16[192,192]{1,0:T(8,128)(2,1)} %kw_hbm.1, ...), custom_call_target="tpu_custom_call" | custom-call | tf_op jit(solution)/shard_map/pallas_call | solution.py:490
  130.1 1.8 %copy.11 = bf16[1,128,1536]{2,1,0:T(8,128)(2,1)} copy(bf16[1,128,1536]{2,1,0:T(8,128)(2,1)} %shard_map.82) | data formatting | bytes 786432

commit v4 on v3

--- a/solution.py
+++ b/solution.py
@@ -116,13 +116,13 @@
         return c
 
     def text_cols(p):
-        return text_hbm.at[0, :, pl.ds(p * 2048, 2048)]
+        return text_hbm.at[0, :, pl.ds(p * 1024, 1024)]
 
     c_kw = local(kw_hbm, kraw)
     c_mod = local(mod_hbm.at[0], mraw)
     cw = [cw_hbm.at[pl.ds(p * 96, 96)] for p in (0, 1)]
     c_cw = [local(cw[0], w0.at[x, core, y]), local(cw[1], w1.at[y, core, x])]
-    c_text = [local(text_cols(p), tx.at[p, z]) for p in (0, 1)]
+    c_text = [local(text_cols(p), tx.at[p, z]) for p in range(4)]
     c_img = [
         local(cols(q_hbm, mine), qb.at[0]),
         local(cols(fresh_hbm, mine), fk.at[0]),
@@ -140,7 +140,10 @@
     mb[h, 0:2, 0:192] = mraw[...]
     pl.semaphore_wait(barrier, len(peers))
 
-    text = [Ring(net, lambda k, p=p: tx.at[p, at_z(k)], p, left, right, text_cols(p), True) for p in (0, 1)]
+    text = [
+        Ring(net, lambda k, p=p: tx.at[p, at_z(k)], p % 2, left, right, text_cols(p), True)
+        for p in range(4)
+    ]
 
     class Spread:
         def __init__(self, buf, i, j, own, first, second):
@@ -225,7 +228,8 @@
                     a, b = tile(w0, w1, i, c, lo)
                     blocks.append(jnp.concatenate([a[0:128], b[0:128], a[128:], b[128:]], axis=0))
             rhs = jnp.concatenate(blocks, axis=1)
-            lhs = tx[i // 2, :, :, (i % 2) * 1024 : (i % 2 + 1) * 1024].reshape(256, 1024)
+            text[i].finish()
+            lhs = tx[i].reshape(256, 1024)
             ctx = ctx + lax.dot_general(
                 lhs, rhs, (((1,), (1,)), ((), ())), preferred_element_type=F32
             )
@@ -233,7 +237,7 @@
         s1 = jnp.sum(ctx, -1, keepdims=True)
         s2 = jnp.sum(ctx * ctx, -1, keepdims=True)
         both = jnp.where(lane == 0, s1, jnp.where(lane == 1, s2, 0.0))
-        st[0] = jnp.transpose(both)[0:8]
+        st[0] = jnp.transpose(both)[0:2]
         st_c = [net.copy(st.at[0], st.at[k], zs[k]) for k in zs]
         for c in st_c:
             c.start()
@@ -251,7 +255,7 @@
         tot = st[0]
         for k in range(1, NZ):
             tot = tot + st[k]
-        tot = jnp.transpose(jnp.concatenate([tot, jnp.zeros((120, 256), F32)], axis=0))
+        tot = jnp.transpose(jnp.concatenate([tot, jnp.zeros((126, 256), F32)], axis=0))
         average = tot[:, 0:1] / D
         variance = tot[:, 1:2] / D - average * average
         normed = (
@@ -445,7 +449,6 @@
         "F1": lambda: finish(1),
         "A0": first,
         "ts": lambda: each(text, "start"),
-        "tf": lambda: each(text, "finish"),
         "af": lambda: each(tring, "finish"),
     }
     for n in range(4):
@@ -476,11 +479,11 @@
     *((s, r, g) for s in (1, 2, 3) for g in (0, 1) for r in (0, 1)),
 )
 PLAN = (
-    "ts", "ws", "ms", "wm", "ks", "so", "t1", "t2", "P", "P", "t3", "wp",
-    "km", "P", "P", "wf", "tf", "T1", "kp", "qf", "P", "P", "NO", "kf",
-    "T2", "r0", "P", "r1", "P", "A0", "r2", "P", "r3", "P", "rf", "P",
-    "to", "S17", "a1", "P", "X017", "a2", "P", "S26", "X26", "a3", "P", "PA",
-    "S35", "af", "X354", "F0", "F1",
+    "ts", "ws", "ms", "wm", "ks", "so", "t1", "t2", "P", "t3", "P", "wp",
+    "km", "P", "P", "wf", "T1", "kp", "qf", "P", "P", "NO", "kf", "T2",
+    "r0", "P", "r1", "P", "A0", "r2", "P", "r3", "P", "rf", "P", "to",
+    "S17", "a1", "P", "X017", "a2", "P", "S26", "X26", "a3", "P", "PA", "S35",
+    "af", "X354", "F0", "F1",
 )
 
 
@@ -493,7 +496,7 @@
         in_specs=[hbm] * 7 + [smem],
         out_specs=hbm,
         scratch_shapes=[
-            pltpu.VMEM((2, NZ, 32, 2048), BF),
+            pltpu.VMEM((4, NZ, 32, 1024), BF),
             pltpu.VMEM((192, 192), BF),
             pltpu.VMEM((288, 128), BF),
             pltpu.VMEM((NX, 2, NY, 96, 256), BF),
@@ -502,7 +505,7 @@
             pltpu.VMEM((NY, 2, NX, 144, 128), BF),
             pltpu.VMEM((2, 192), F32),
             pltpu.VMEM((2, 8, 256), F32),
-            pltpu.VMEM((NZ, 8, 256), F32),
+            pltpu.VMEM((NZ, 2, 256), F32),
             pltpu.VMEM((NZ, 32, D), F32),
             pltpu.VMEM((2, 4, 2, 32, D // 2), BF),
             pltpu.VMEM((2, 4, 2, 32, D // 2), BF),

time: 132 us -> 131 us (level)
  no operation moved by 1% of the time
where the time goes in v4:
time: 131 us
  Pallas kernels  128 us (98%)
  local copies, waits for them, and re-layouts  1.77 us (1%)
    pallas_call x1, Pallas kernels, per_device(): pl.pallas_call(kernel, out_shape=jax.ShapeDtypeStruct((1, 128, 1536), BF)...  128 us

profile of v4, /device:TPU:2, one launch (start us, length us, event | category | flops | bytes accessed | tf_op | source)
XLA Modules:
  0.0 130.9 jit_solution(14085085673423579461)
XLA Ops:
  0.7 128.4 %shard_map.82 = bf16[1,128,1536]{2,1,0:T(8,128)(2,1)} custom-call(bf16[1,128,1536]{2,1,0:T(8,128)(2,1)} %q_hbm.1, bf16[1,128,3072]{2,1,0:T(8,128)(2,1)} %fresh_hbm.1, bf16[1,128,3072]{2,1,0:T(8,128)(2,1)} %stale_hbm.1, bf16[1,32,4096]{2,1,0:T(8,128)(2,1)} %text_hbm.1, bf16[192,256]{1,0:T(8,128)(2,1)} %bitcast.1, bf16[192,192]{1,0:T(8,128)(2,1)} %kw_hbm.1, ...), custom_call_target="tpu_custom_call" | custom-call | tf_op jit(solution)/shard_map/pallas_call | solution.py:493
  129.1 1.8 %copy.11 = bf16[1,128,1536]{2,1,0:T(8,128)(2,1)} copy(bf16[1,128,1536]{2,1,0:T(8,128)(2,1)} %shard_map.82) | data formatting | bytes 786432

commit v5 on v4

--- a/solution.py
+++ b/solution.py
@@ -138,10 +138,12 @@
     k1[y, core, x] = kpack[144:288]
     c_mod.wait()
     mb[h, 0:2, 0:192] = mraw[...]
+    for c in (*c_text, *c_img):
+        c.wait()
     pl.semaphore_wait(barrier, len(peers))
 
     text = [
-        Ring(net, lambda k, p=p: tx.at[p, at_z(k)], p % 2, left, right, text_cols(p), True)
+        Ring(net, lambda k, p=p: tx.at[p, at_z(k)], p % 2, left, right, by_origin=True)
         for p in range(4)
     ]
 
@@ -189,8 +191,7 @@
     ]
     stale = {
         (r, g, v): Ring(
-            net, lambda k, b=b, r=r, g=g: b.at[g, k, r], v, left, right,
-            None if r else group(mine, g, v),
+            net, lambda k, b=b, r=r, g=g: b.at[g, k, r], v, left, right
         )
         for r in (0, 1)
         for g in (0, 1)
@@ -219,7 +220,6 @@
     held = {}
 
     def context():
-        each(c_text, "wait")
         ctx = jnp.zeros((256, 384), F32)
         for i in range(NX):
             blocks = []
@@ -390,7 +390,6 @@
         )
 
     def first():
-        each(c_img, "wait")
         each(qf_opp, "wait_recv")
         for g in (0, 1):
             for n in range(3 * g, 3 * g + 3):

time: 131 us -> 131 us (level)
  no operation moved by 1% of the time
where the time goes in v5:
time: 131 us
  Pallas kernels  128 us (98%)
  local copies, waits for them, and re-layouts  1.77 us (1%)
    pallas_call x1, Pallas kernels, per_device(): pl.pallas_call(kernel, out_shape=jax.ShapeDtypeStruct((1, 128, 1536), BF)...  128 us

profile of v5, /device:TPU:2, one launch (start us, length us, event | category | flops | bytes accessed | tf_op | source)
XLA Modules:
  0.0 130.7 jit_solution(14999974554708588522)
XLA Ops:
  0.7 128.2 %shard_map.82 = bf16[1,128,1536]{2,1,0:T(8,128)(2,1)} custom-call(bf16[1,128,1536]{2,1,0:T(8,128)(2,1)} %q_hbm.1, bf16[1,128,3072]{2,1,0:T(8,128)(2,1)} %fresh_hbm.1, bf16[1,128,3072]{2,1,0:T(8,128)(2,1)} %stale_hbm.1, bf16[1,32,4096]{2,1,0:T(8,128)(2,1)} %text_hbm.1, bf16[192,256]{1,0:T(8,128)(2,1)} %bitcast.1, bf16[192,192]{1,0:T(8,128)(2,1)} %kw_hbm.1, ...), custom_call_target="tpu_custom_call" | custom-call | tf_op jit(solution)/shard_map/pallas_call | solution.py:492
  128.9 1.8 %copy.11 = bf16[1,128,1536]{2,1,0:T(8,128)(2,1)} copy(bf16[1,128,1536]{2,1,0:T(8,128)(2,1)} %shard_map.82) | data formatting | bytes 786432
